TPU v7x, 32 devices: a whole 2x2x4 slice. The times are simulated.
32 devices in a mesh: groups: 2 (over y), patch: 8 (over z, x), visit: 2 (over core).
Axes of the slice: x: 2, y: 2, z: 4, core: 2. Of those that a mesh axis runs over, the one named last changes fastest.
Arguments:
- visit_tiles: bfloat16 [1792, 64, 1024], P(('groups', 'patch', 'visit')), parts along dimension 0, may hold values from -6 to 6
- tile_patch: int32 [1792], P(('groups', 'patch', 'visit')), parts along dimension 0, may hold values from 0 to 7, as said below
- offsets: int32 [1792, 2], P(('groups', 'patch', 'visit')), parts along dimension 0, may hold values from -128 to 127
- psf_coefs: int32 [1792, 3], P(('groups', 'patch', 'visit')), parts along dimension 0, may hold values from 16 to 80
- weights: bfloat16 [1792], P(('groups', 'patch', 'visit')), parts along dimension 0, may hold values from 0.19921875 to 4
Outputs:
- coadd: float32 [1024, 1024], P(('groups', 'patch')), parts along dimension 0
- detection: float32 [1024, 1024], P(('groups', 'patch')), parts along dimension 0
There are 2 independent parts, one for each index of `groups`. A program takes and returns all parts, laid end to end along the dimension named above; each array names one. Nothing has to cross between parts.
Inputs may be any that keep to these rules, and one draw needn't show every extreme that they name: `tile_patch`: among the 56 tiles of one device at most 14 name any one patch; 2 deep-field patches are named by exactly 14 tiles of every device; every patch is named by some tile.
All inputs are finite; a program needn't handle non-finite values.
Results may differ from a plain program's by a relative error of at most 0.0048.
Values may be sent and summed in bfloat16 or wider, within the bound.
A program may use at most 128 MiB of HBM per device.

v0:
```python
import functools
import math

import jax
import jax.numpy as jnp
import numpy as np
from jax import lax
from jax.experimental import pallas as pl
from jax.experimental.pallas import tpu as pltpu
from jax.sharding import PartitionSpec as P

HALO = 8
PSF_SIGMAS = (0.75, 1.5, 3.0)
PSF_REACH = 16
MID = 5
LANES = 128
HALF = 64
MESH = pl.DeviceIdType.MESH
BF16 = jnp.bfloat16
F32 = jnp.float32


def gaussian_taps(sigma, reach):
    distance = np.arange(-reach, reach + 1, dtype=np.float64)
    return np.exp(-distance * distance / (2.0 * sigma * sigma)) / (math.pi * sigma * sigma) ** 0.25


def well_rounded_scale(sigma, reach):
    taps = gaussian_taps(sigma, reach)
    scales = 1.0 + np.arange(1024) / 1024.0
    scaled = taps[None, :] * scales[:, None]
    rounded = scaled.astype(np.float32).astype(BF16).astype(np.float64)
    error = np.sum((rounded - scaled) ** 2, axis=1) / scales**2
    gain = (np.sum(rounded - scaled, axis=1) / scales) ** 2
    return float(scales[np.argmin(error + gain)])


def gaussian(distance, sigma, reach, scale):
    distance = distance.astype(F32)
    shape = jnp.exp(distance * distance * (-0.5 / (sigma * sigma))) * (scale / (math.pi * sigma * sigma) ** 0.25)
    return jnp.where(jnp.abs(distance) <= reach, shape, 0.0)


def row_minus_col(shape):
    return lax.broadcasted_iota(jnp.int32, shape, 0) - lax.broadcasted_iota(jnp.int32, shape, 1)


def split_high_low(matrix):
    high = matrix.astype(BF16)
    return high, (matrix - high.astype(F32)).astype(BF16)


def sinc(value):
    angle = jnp.where(value == 0.0, 1.0, math.pi * value)
    return jnp.where(value == 0.0, 1.0, jnp.sin(angle) / angle)


def lanczos(value):
    inside = jnp.abs(value) < 3.0
    value = jnp.where(inside, value, 0.0)
    return jnp.where(inside, sinc(value) * sinc(value / 3.0), 0.0)


LOW, HIGH = HALF - 16, HALF + LANES + 16


def column_warp(tile, table_row):
    rows, cols = tile.shape
    shape = (HIGH - LOW, LANES)
    band = pltpu.roll(jnp.broadcast_to(table_row, shape), 0, axis=1, stride=1, stride_axis=0)
    distance = row_minus_col(shape) - (HALF - LOW)
    band = jnp.where(jnp.abs(distance) <= MID, band, 0.0).astype(BF16)
    matrix = jnp.concatenate([jnp.zeros((LOW, LANES), BF16), band, jnp.zeros((2 * LANES - HIGH, LANES), BF16)], axis=0)
    edge = jnp.zeros((rows, LANES), BF16)
    padded = jnp.concatenate([edge, tile, edge], axis=1)
    blocks = cols // LANES + 1
    windows = jnp.concatenate([padded[:, m * LANES : (m + 2) * LANES] for m in range(blocks)], axis=0)
    return jnp.dot(windows, matrix, preferred_element_type=F32).astype(BF16)


def row_matrices(table_rows, factors, g_rows, rows):
    shape = (rows, LANES)
    per = LANES // rows
    lane_slot = lax.broadcasted_iota(jnp.int32, shape, 1) // rows
    shifts = []
    for first in range(0, len(table_rows), per):
        both = jnp.zeros(shape, F32)
        for s in range(per):
            row = jnp.broadcast_to(table_rows[first + s], shape)
            band = pltpu.roll(row, s * rows, axis=1, stride=1, stride_axis=0)
            both = jnp.where(lane_slot == s, band, both)
        shifts.append(both.astype(BF16))
    shift = jnp.concatenate(shifts, axis=1)
    blurred = jnp.dot(g_rows, jnp.concatenate([shift, shift], axis=0), preferred_element_type=F32)
    pieces = []
    for k in range(3):
        factor = factors[k : k + 1, :] + factors[3 + k : 4 + k, :]
        pieces.append(blurred[k * rows : (k + 1) * rows] * factor)
    return jnp.concatenate(pieces, axis=0).astype(BF16)


def detect(coadd, before, after):
    rows, cols = coadd.shape
    sigma = HALO / 4.0
    scale = well_rounded_scale(sigma, HALO)
    extended = jnp.concatenate([before, coadd, after], axis=0)
    h_rows = gaussian(row_minus_col((rows, rows + 2 * HALO)) + HALO, sigma, HALO, 1.0 / scale)
    blurred = jnp.dot(h_rows, extended, preferred_element_type=F32, precision=lax.Precision.HIGHEST).astype(BF16)
    h_cols = gaussian(row_minus_col((3 * LANES, LANES)) - LANES, sigma, HALO, scale).astype(BF16)
    edge = jnp.zeros((rows, LANES), BF16)
    padded = jnp.concatenate([edge, blurred, edge], axis=1)
    windows = jnp.concatenate([padded[:, m * LANES : (m + 3) * LANES] for m in range(cols // LANES)], axis=0)
    result = jnp.dot(windows, h_cols, preferred_element_type=F32)
    return jnp.concatenate([result[m * rows : (m + 1) * rows] for m in range(cols // LANES)], axis=1)


def slot_tables(named, offsets, coefs, weights, owners, capacity):
    count = named.shape[1]
    slots = owners * capacity
    square = (count, count)
    sublane, lane = lax.broadcasted_iota(jnp.int32, square, 0), lax.broadcasted_iota(jnp.int32, square, 1)

    def to_column(row):
        spread = jnp.where(sublane == lane, jnp.broadcast_to(row, square), jnp.zeros(square, row.dtype))
        return jnp.sum(spread, axis=1, keepdims=True)

    named_column = to_column(named)
    same = jnp.where(jnp.broadcast_to(named, square) == jnp.broadcast_to(named_column, square), 1, 0)
    rank_row = jnp.sum(jnp.where(sublane < lane, same, 0), axis=0, keepdims=True)
    rank_column = jnp.sum(jnp.where(lane < sublane, same, 0), axis=1, keepdims=True)
    slot_row = named * capacity + rank_row
    slot_column = named_column * capacity + rank_column

    chosen = lax.broadcasted_iota(jnp.int32, (slots, count), 0) == slot_row
    place = lax.broadcasted_iota(jnp.int32, (count, slots), 1) == slot_column
    tile = lax.broadcasted_iota(jnp.int32, (count, slots), 0)
    source = jnp.sum(jnp.where(place, tile, 0), axis=0, keepdims=True)

    shift = offsets.astype(F32) / 64.0
    at = lax.broadcasted_iota(jnp.int32, (count, LANES), 1)
    col_table = lanczos((at - LANES + HALF - LOW).astype(F32) + to_column(shift[1:2]))
    col_table = col_table.astype(BF16).astype(F32)
    row_table = lanczos(jnp.where(at < HALF, -at, LANES - at).astype(F32) + to_column(shift[0:1]))
    one = jnp.where(chosen, 1.0, 0.0).astype(BF16)
    row_table = jnp.dot(one, row_table.astype(BF16), preferred_element_type=F32)
    factor = weights * (coefs.astype(F32) / 64.0)
    high, low = split_high_low(factor)
    rest = jnp.zeros((2, count), F32)
    factors = jnp.concatenate([high.astype(F32), low.astype(F32), rest], axis=0).astype(BF16)
    return col_table, row_table, factors, slot_column, source


def fused_kernel(
    owners, capacity, chunk,
    tiles_hbm, args_ref, weight_ref,
    coadd_ref, detection_ref,
    tiles, warped, blur_even, blur_odd, left_even, left_odd, part, g_rows, g_cols, load_sems,
    col_table, row_table, factor_rows, slot_column, w_part, source_row, source, source_sem,
    pair_in, sums, arrived, w_pair, w_sums, w_arrived, halos,
    pair_send, pair_recv, w_pair_sems, send, recv, w_send, w_recv, last_sems, halo_send, halo_recv,
):
    me, core = lax.axis_index("patch"), lax.axis_index("visit")
    other = 1 - core
    count, rows, cols = tiles.shape
    wide = cols + LANES
    half = rows // 2
    chunks = count // chunk
    mine, theirs = pl.ds(core * half, half), pl.ds(other * half, half)

    def load(c):
        span = pl.ds(c * chunk, chunk)
        return pltpu.make_async_copy(tiles_hbm.at[span], tiles.at[span], load_sems.at[c])

    for c in range(chunks):
        load(c).start()

    barrier = pltpu.get_barrier_semaphore()

    def greet(i, carry):
        flat = (me * 2 + core + i) % (2 * owners)
        pl.semaphore_signal(barrier, inc=1, device_id={"patch": flat // 2, "visit": flat % 2}, device_id_type=MESH)
        return carry

    lax.fori_loop(1, 2 * owners, greet, 0)

    for k, sigma in enumerate(PSF_SIGMAS):
        scale = well_rounded_scale(sigma, PSF_REACH)
        high, low = split_high_low(gaussian(row_minus_col((rows, rows)), sigma, PSF_REACH, 1.0 / scale))
        g_rows[k * rows : (k + 1) * rows] = jnp.concatenate([high, low], axis=1)
        taps = gaussian(row_minus_col((2 * LANES, LANES)) - HALF, sigma, PSF_REACH, scale)
        g_cols[2 * k * LANES : 2 * (k + 1) * LANES] = taps.astype(BF16)

    args = args_ref[...]
    named, weight = args[0:1], weight_ref[...]
    col_values, row_values, factor_values, column, row = slot_tables(
        named, args[1:3], args[3:6], weight, owners, capacity
    )
    source_row[...] = row
    source_copy = pltpu.make_async_copy(source_row, source, source_sem)
    source_copy.start()
    col_table[...] = col_values
    row_table[...] = row_values
    factor_rows[...] = factor_values
    slot_column[...] = column
    for p in range(owners):
        here = jnp.where(named == p, weight * weight, 0.0)
        w_part[p] = jnp.broadcast_to(jnp.sum(here, axis=1, keepdims=True), (8, LANES))

    def warp_chunk(c, carry):
        load(c).wait()

        def warp(step, carry):
            v = c * chunk + step
            result = column_warp(tiles[v], col_table[pl.ds(v, 1), :])
            for m in range(wide // LANES):
                warped[v, :, m * LANES : (m + 1) * LANES] = result[m * rows : (m + 1) * rows]
            return carry

        return lax.fori_loop(0, chunk, warp, carry, unroll=chunk)

    lax.fori_loop(0, chunks, warp_chunk, 0)
    source_copy.wait()

    pl.semaphore_wait(barrier, 2 * owners - 1)

    def pair_copy(q):
        return pltpu.make_async_remote_copy(
            part.at[q, theirs], pair_in.at[q], pair_send.at[q], pair_recv.at[q],
            device_id={"visit": other}, device_id_type=MESH,
        )

    w_copy = pltpu.make_async_remote_copy(
        w_part, w_pair, w_pair_sems.at[0], w_pair_sems.at[1], device_id={"visit": other}, device_id_type=MESH
    )

    def out_copy(q, slot):
        return pltpu.make_async_remote_copy(
            sums.at[q], arrived.at[slot], send.at[q], recv.at[slot], device_id={"patch": q}, device_id_type=MESH
        )

    def w_out_copy(q, slot):
        return pltpu.make_async_remote_copy(
            w_sums.at[q], w_arrived.at[slot], w_send.at[q], w_recv.at[slot], device_id={"patch": q}, device_id_type=MESH
        )

    w_copy.start()

    depth = capacity * rows
    pieces = [(a, min(a + 2 * LANES, wide)) for a in range(0, wide, 2 * LANES)]

    lefts, blurs = (left_even, left_odd), (blur_even, blur_odd)

    def owner(i):
        return (me + i) % owners

    def prepare(i, parity):
        p = owner(i)
        lane_slot = p * capacity + lax.broadcasted_iota(jnp.int32, (count, depth), 1) // rows
        spread = jnp.where(slot_column[...] == lane_slot, 1.0, 0.0).astype(BF16)
        factors = jnp.dot(factor_rows[...], spread, preferred_element_type=F32)
        table_rows = [row_table[pl.ds(p * capacity + r, 1), :] for r in range(capacity)]
        lefts[parity][...] = row_matrices(table_rows, factors, g_rows[...], rows)

    def stack(i, parity):
        p = owner(i)
        slots = [jnp.clip(source[0, p * capacity + r], 0, count - 1) for r in range(capacity)]
        for a, b in pieces:
            right = jnp.concatenate([warped[s, :, a:b] for s in slots], axis=0)
            total = jnp.dot(lefts[parity][...], right, preferred_element_type=F32)
            lane = a + lax.broadcasted_iota(jnp.int32, total.shape, 1)
            if a < HALF or b > wide - HALF:
                total = jnp.where((lane >= HALF) & (lane < wide - HALF), total, 0.0)
            blurs[parity][:, a:b] = total.astype(BF16)

    def match(i, parity):
        p, blur = owner(i), blurs[parity]
        windows = jnp.concatenate(
            [
                jnp.concatenate([blur[k * rows : (k + 1) * rows, m * LANES : (m + 2) * LANES] for k in range(3)], axis=1)
                for m in range(cols // LANES)
            ],
            axis=0,
        )
        result = jnp.dot(windows, g_cols[...], preferred_element_type=F32).astype(BF16)
        for m in range(cols // LANES):
            part[p, :, m * LANES : (m + 1) * LANES] = result[m * rows : (m + 1) * rows]

    def forward(q):
        pair_copy(q).wait()
        sums[q] = (part[q, mine].astype(F32) + pair_in[q].astype(F32)).astype(BF16)
        out_copy(q, me).start()
        w_out_copy(q, me).start()

    prepare(1, 1)
    prepare(2, 0)
    stack(1, 1)
    w_copy.wait()
    w_sums[...] = w_part[...] + w_pair[...]

    def step(i, parity):
        prepare(i + 1, 1 - parity)
        match(i - 1, 1 - parity)
        stack(i, parity)
        pair_copy(owner(i - 1)).start()

    step(2, 0)

    def two_patches(j, carry):
        step(2 * j + 1, 1)
        forward(owner(2 * j - 1))
        step(2 * j + 2, 0)
        forward(owner(2 * j))
        return carry

    lax.fori_loop(1, owners // 2, two_patches, 0)
    match(owners, 0)
    pair_copy(me).start()
    forward(owner(owners - 1))
    pair_copy(me).wait()
    total = part[me, mine].astype(F32) + pair_in[me].astype(F32)

    def collect(i, carry):
        total, weight = carry
        q = (me + owners - i) % owners
        out_copy(q, q).wait_recv()
        w_out_copy(q, q).wait_recv()
        return total + arrived[q].astype(F32), weight + w_arrived[q]

    total, weight = lax.fori_loop(1, owners, collect, (total, w_sums[me]))
    coadd_ref[mine] = total / jnp.sqrt(weight[0:1, 0:1])

    last = pltpu.make_async_remote_copy(
        coadd_ref.at[mine], coadd_ref.at[mine], last_sems.at[0], last_sems.at[1],
        device_id={"visit": other}, device_id_type=MESH,
    )
    last.start()
    neighbour = (me + owners - 1 + 2 * core) % owners
    border = pl.ds(core * (rows - HALO), HALO)

    def halo_copy(to):
        return pltpu.make_async_remote_copy(
            coadd_ref.at[border], halos.at[other], halo_send.at[to], halo_recv.at[other],
            device_id={"patch": neighbour, "visit": to}, device_id_type=MESH,
        )

    for to in range(2):
        halo_copy(to).start()

    def finish(i, carry):
        q = (me + i) % owners
        out_copy(q, me).wait_send()
        w_out_copy(q, me).wait_send()
        return carry

    lax.fori_loop(1, owners, finish, 0)
    for to in range(2):
        halo_copy(to).wait_send()
    for side in range(2):
        pltpu.make_async_remote_copy(
            coadd_ref.at[border], halos.at[side], halo_send.at[0], halo_recv.at[side],
            device_id={"patch": neighbour, "visit": other}, device_id_type=MESH,
        ).wait_recv()
    last.wait()
    before = jnp.where(me > 0, halos[0], 0.0)
    after = jnp.where(me < owners - 1, halos[1], 0.0)
    detection_ref[...] = detect(coadd_ref[...], before, after)


def shards(visit_tiles, tile_patch, offsets, psf_coefs, weights):
    count, rows, cols = visit_tiles.shape
    owners = lax.axis_size("patch")
    capacity = max(2, 2 * count // owners)
    capacity += capacity % 2
    chunk = math.gcd(count, 8)
    wide = cols + LANES
    half = rows // 2
    args, first = jnp.zeros((8, count), jnp.int32), 0
    for array in (tile_patch[None, :], offsets.T, psf_coefs.T):
        last = first + array.shape[0]
        args = args + jnp.pad(array, ((first, 8 - last), (0, 0)))
        first = last
    vmem = pl.BlockSpec(memory_space=pltpu.VMEM)
    hbm = pl.BlockSpec(memory_space=pltpu.HBM)
    dma = pltpu.SemaphoreType.DMA
    return pl.pallas_call(
        functools.partial(fused_kernel, owners, capacity, chunk),
        out_shape=(jax.ShapeDtypeStruct((rows, cols), F32), jax.ShapeDtypeStruct((rows, cols), F32)),
        in_specs=[hbm, vmem, vmem],
        out_specs=(vmem, vmem),
        scratch_shapes=[
            pltpu.VMEM((count, rows, cols), BF16),
            pltpu.VMEM((count, rows, wide), BF16),
            pltpu.VMEM((3 * rows, wide), BF16),
            pltpu.VMEM((3 * rows, wide), BF16),
            pltpu.VMEM((3 * rows, capacity * rows), BF16),
            pltpu.VMEM((3 * rows, capacity * rows), BF16),
            pltpu.VMEM((owners, rows, cols), BF16),
            pltpu.VMEM((3 * rows, 2 * rows), BF16),
            pltpu.VMEM((6 * LANES, LANES), BF16),
            dma((count // chunk,)),
            pltpu.VMEM((count, LANES), F32),
            pltpu.VMEM((owners * capacity, LANES), F32),
            pltpu.VMEM((8, count), BF16),
            pltpu.VMEM((count, 1), jnp.int32),
            pltpu.VMEM((owners, 8, LANES), F32),
            pltpu.VMEM((1, owners * capacity), jnp.int32),
            pltpu.SMEM((1, owners * capacity), jnp.int32),
            dma(()),
            pltpu.VMEM((owners, half, cols), BF16),
            pltpu.VMEM((owners, half, cols), BF16),
            pltpu.VMEM((owners, half, cols), BF16),
            pltpu.VMEM((owners, 8, LANES), F32),
            pltpu.VMEM((owners, 8, LANES), F32),
            pltpu.VMEM((owners, 8, LANES), F32),
            pltpu.VMEM((2, HALO, cols), F32),
            dma((owners,)), dma((owners,)), dma((2,)),
            dma((owners,)), dma((owners,)), dma((owners,)), dma((owners,)),
            dma((2,)), dma((2,)), dma((2,)),
        ],
        compiler_params=pltpu.CompilerParams(
            collective_id=0, has_side_effects=True, vmem_limit_bytes=52 * 2**20
        ),
        name="fused",
    )(visit_tiles, args, weights.astype(F32)[None, :])


def solution(mesh):
    placed = (
        P(("groups", "patch", "visit"), None, None),
        P(("groups", "patch", "visit")),
        P(("groups", "patch", "visit"), None),
        P(("groups", "patch", "visit"), None),
        P(("groups", "patch", "visit")),
    )
    return jax.shard_map(
        shards,
        mesh=mesh,
        in_specs=placed,
        out_specs=(P(("groups", "patch"), None), P(("groups", "patch"), None)),
        check_vma=False,
    )
```

profile of v0, /device:TPU:0, one launch (start us, length us, event | category | flops | bytes accessed | tf_op | source)
XLA Modules:
  0.0 36.3 jit_solution(11208680425628276377)
XLA Ops:
  0.6 0.7 %bitcast_convert_fusion.weight_ref = f32[1,56]{1,0:T(1,128)S(1)} fusion(bf16[56]{0:T(256)(128)(2,1)} %param.9), kind=kLoop, calls=%fused_computation.1 | loop fusion | flops 56 | bytes 336 | tf_op jit(solution)/shard_map/broadcast_in_dim | solution.py:424
  1.3 0.7 %pad_add_fusion.args_ref = s32[8,56]{1,0:T(8,128)S(1)} fusion(s32[3,56]{1,0:T(4,128)} %bitcast.6, s32[2,56]{1,0:T(2,128)} %bitcast.7, s32[1,56]{1,0:T(1,128)} %bitcast.8), kind=kLoop, calls=%fused_computation | loop fusion | flops 896 | bytes 3136 | tf_op jit(solution)/shard_map/add | solution.py:380
  2.0 32.9 %fused.1 = (f32[64,1024]{1,0:T(8,128)S(1)}, f32[64,1024]{1,0:T(8,128)S(1)}) custom-call(bf16[56,64,1024]{2,1,0:T(8,128)(2,1)} %tiles_hbm.1, s32[8,56]{1,0:T(8,128)S(1)} %pad_add_fusion.args_ref, f32[1,56]{1,0:T(1,128)S(1)} %bitcast_convert_fusion.weight_ref), custom_call_target="tpu_custom_call" | custom-call | tf_op jit(solution)/shard_map/fused/pallas_call | solution.py:385
  34.9 0.7 %copy.9 = f32[64,1024]{1,0:T(8,128)} copy(f32[64,1024]{1,0:T(8,128)S(1)} %get-tuple-element.4) | data formatting | bytes 524288
  35.6 0.7 %copy.10 = f32[64,1024]{1,0:T(8,128)} copy(f32[64,1024]{1,0:T(8,128)S(1)} %get-tuple-element.5) | data formatting | bytes 524288
where the time goes:
time: 36.5 us; the launch traced here: 36.3 us
  Pallas kernels  32.9 us (90%)
  local copies, waits for them, and re-layouts  1.41 us (4%)
  other arithmetic  1.37 us (4%)
  between operations  0.64 us (2%)
    pallas_call x1, Pallas kernels, shards(): pl.pallas_call(functools.partial(fused_kernel, owners, capacity, chunk),...  32.9 us
    unnamed x2, local copies, waits for them, and re-layouts  1.41 us

commit v1 on v0

--- a/solution.py
+++ b/solution.py
@@ -153,7 +153,7 @@
 def fused_kernel(
     owners, capacity, chunk,
     tiles_hbm, args_ref, weight_ref,
-    coadd_ref, detection_ref,
+    out_ref,
     tiles, warped, blur_even, blur_odd, left_even, left_odd, part, g_rows, g_cols, load_sems,
     col_table, row_table, factor_rows, slot_column, w_part, source_row, source, source_sem,
     pair_in, sums, arrived, w_pair, w_sums, w_arrived, halos,
@@ -165,6 +165,7 @@
     wide = cols + LANES
     half = rows // 2
     chunks = count // chunk
+    coadd_ref = out_ref.at[0]
     mine, theirs = pl.ds(core * half, half), pl.ds(other * half, half)
 
     def load(c):
@@ -297,25 +298,23 @@
     w_copy.wait()
     w_sums[...] = w_part[...] + w_pair[...]
 
-    def step(i, parity):
-        prepare(i + 1, 1 - parity)
+    def step(i, parity, last=False):
+        if not last:
+            prepare(i + 1, 1 - parity)
         match(i - 1, 1 - parity)
+        pair_copy(owner(i - 1)).start()
         stack(i, parity)
-        pair_copy(owner(i - 1)).start()
-
-    step(2, 0)
+        forward(owner(i - 1))
 
     def two_patches(j, carry):
+        step(2 * j, 0)
         step(2 * j + 1, 1)
-        forward(owner(2 * j - 1))
-        step(2 * j + 2, 0)
-        forward(owner(2 * j))
         return carry
 
     lax.fori_loop(1, owners // 2, two_patches, 0)
+    step(owners, 0, last=True)
     match(owners, 0)
     pair_copy(me).start()
-    forward(owner(owners - 1))
     pair_copy(me).wait()
     total = part[me, mine].astype(F32) + pair_in[me].astype(F32)
 
@@ -363,7 +362,7 @@
     last.wait()
     before = jnp.where(me > 0, halos[0], 0.0)
     after = jnp.where(me < owners - 1, halos[1], 0.0)
-    detection_ref[...] = detect(coadd_ref[...], before, after)
+    out_ref[1] = detect(coadd_ref[...], before, after)
 
 
 def shards(visit_tiles, tile_patch, offsets, psf_coefs, weights):
@@ -382,11 +381,11 @@
     vmem = pl.BlockSpec(memory_space=pltpu.VMEM)
     hbm = pl.BlockSpec(memory_space=pltpu.HBM)
     dma = pltpu.SemaphoreType.DMA
-    return pl.pallas_call(
+    both = pl.pallas_call(
         functools.partial(fused_kernel, owners, capacity, chunk),
-        out_shape=(jax.ShapeDtypeStruct((rows, cols), F32), jax.ShapeDtypeStruct((rows, cols), F32)),
+        out_shape=jax.ShapeDtypeStruct((2, rows, cols), F32),
         in_specs=[hbm, vmem, vmem],
-        out_specs=(vmem, vmem),
+        out_specs=vmem,
         scratch_shapes=[
             pltpu.VMEM((count, rows, cols), BF16),
             pltpu.VMEM((count, rows, wide), BF16),
@@ -422,6 +421,7 @@
         ),
         name="fused",
     )(visit_tiles, args, weights.astype(F32)[None, :])
+    return both[0], both[1]
 
 
 def solution(mesh):

time: 36.5 us -> 36.7 us (level)
  Pallas kernels: 32.9 us -> 33.7 us
  local copies, waits for them, and re-layouts: 1.41 us -> 0.83 us
    unnamed x2 -> x0, local copies, waits for them, and re-layouts: 1.41 us -> none
    squeeze x0 -> x1, local copies, waits for them, and re-layouts: none -> 0.83 us  [shards(): return (both[0], both[1])]
    pallas_call x1, Pallas kernels: 32.9 us -> 33.7 us  [shards(): pl.pallas_call(functools.partial(fused_kernel, owners, capacity, chunk),...]
where the time goes in v1:
time: 36.7 us; the launch traced here: 36.5 us
  Pallas kernels  33.7 us (92%)
  other arithmetic  1.37 us (4%)
  local copies, waits for them, and re-layouts  0.83 us (2%)
  between operations  0.64 us (2%)
    pallas_call x1, Pallas kernels, shards(): pl.pallas_call(functools.partial(fused_kernel, owners, capacity, chunk),...  33.7 us
    squeeze x1, local copies, waits for them, and re-layouts, shards(): return (both[0], both[1])  0.83 us

profile of v1, /device:TPU:0, one launch (start us, length us, event | category | flops | bytes accessed | tf_op | source)
XLA Modules:
  0.0 36.5 jit_solution(13685683779971511963)
XLA Ops:
  0.6 0.7 %bitcast_convert_fusion.weight_ref = f32[1,56]{1,0:T(1,128)S(1)} fusion(bf16[56]{0:T(256)(128)(2,1)} %param.9), kind=kLoop, calls=%fused_computation.3 | loop fusion | flops 56 | bytes 336 | tf_op jit(solution)/shard_map/broadcast_in_dim | solution.py:423
  1.3 0.7 %pad_add_fusion.args_ref = s32[8,56]{1,0:T(8,128)S(1)} fusion(s32[3,56]{1,0:T(4,128)} %bitcast.10, s32[2,56]{1,0:T(2,128)} %bitcast.11, s32[1,56]{1,0:T(1,128)} %bitcast.12), kind=kLoop, calls=%fused_computation.2 | loop fusion | flops 896 | bytes 3136 | tf_op jit(solution)/shard_map/add | solution.py:379
  2.0 33.7 %fused.1 = f32[2,64,1024]{2,1,0:T(8,128)S(1)} custom-call(bf16[56,64,1024]{2,1,0:T(8,128)(2,1)} %tiles_hbm.1, s32[8,56]{1,0:T(8,128)S(1)} %pad_add_fusion.args_ref, f32[1,56]{1,0:T(1,128)S(1)} %bitcast_convert_fusion.weight_ref), custom_call_target="tpu_custom_call" | custom-call | tf_op jit(solution)/shard_map/fused/pallas_call | solution.py:384
  35.7 0.8 %slice_bitcast_fusion = (f32[64,1024]{1,0:T(8,128)}, f32[64,1024]{1,0:T(8,128)}) fusion(f32[2,64,1024]{2,1,0:T(8,128)S(1)} %fused.1), kind=kLoop, calls=%fused_computation | loop fusion | bytes 1048576 | tf_op jit(solution)/shard_map/squeeze | solution.py:424

commit v2 on v1

--- a/solution.py
+++ b/solution.py
@@ -302,19 +302,26 @@
         if not last:
             prepare(i + 1, 1 - parity)
         match(i - 1, 1 - parity)
+        stack(i, parity)
         pair_copy(owner(i - 1)).start()
-        stack(i, parity)
-        forward(owner(i - 1))
+
+    step(2, 0)
 
     def two_patches(j, carry):
-        step(2 * j, 0)
         step(2 * j + 1, 1)
+        forward(owner(2 * j - 1))
+        step(2 * j + 2, 0)
+        forward(owner(2 * j))
         return carry
 
-    lax.fori_loop(1, owners // 2, two_patches, 0)
+    lax.fori_loop(1, owners // 2 - 1, two_patches, 0)
+    step(owners - 1, 1)
+    forward(owner(owners - 3))
     step(owners, 0, last=True)
+    forward(owner(owners - 2))
     match(owners, 0)
     pair_copy(me).start()
+    forward(owner(owners - 1))
     pair_copy(me).wait()
     total = part[me, mine].astype(F32) + pair_in[me].astype(F32)
 

time: 36.7 us -> 35.9 us (0.978)
  Pallas kernels: 33.7 us -> 32.9 us
    pallas_call x1, Pallas kernels: 33.7 us -> 32.9 us  [shards(): pl.pallas_call(functools.partial(fused_kernel, owners, capacity, chunk),...]
where the time goes in v2:
time: 35.9 us; the launch traced here: 35.8 us
  Pallas kernels  32.9 us (92%)
  other arithmetic  1.37 us (4%)
  local copies, waits for them, and re-layouts  0.83 us (2%)
  between operations  0.64 us (2%)
    pallas_call x1, Pallas kernels, shards(): pl.pallas_call(functools.partial(fused_kernel, owners, capacity, chunk),...  32.9 us
    squeeze x1, local copies, waits for them, and re-layouts, shards(): return (both[0], both[1])  0.83 us

profile of v2, /device:TPU:0, one launch (start us, length us, event | category | flops | bytes accessed | tf_op | source)
XLA Modules:
  0.0 35.8 jit_solution(6030312714785536653)
XLA Ops:
  0.6 0.7 %bitcast_convert_fusion.weight_ref = f32[1,56]{1,0:T(1,128)S(1)} fusion(bf16[56]{0:T(256)(128)(2,1)} %param.9), kind=kLoop, calls=%fused_computation.3 | loop fusion | flops 56 | bytes 336 | tf_op jit(solution)/shard_map/broadcast_in_dim | solution.py:430
  1.3 0.7 %pad_add_fusion.args_ref = s32[8,56]{1,0:T(8,128)S(1)} fusion(s32[3,56]{1,0:T(4,128)} %bitcast.10, s32[2,56]{1,0:T(2,128)} %bitcast.11, s32[1,56]{1,0:T(1,128)} %bitcast.12), kind=kLoop, calls=%fused_computation.2 | loop fusion | flops 896 | bytes 3136 | tf_op jit(solution)/shard_map/add | solution.py:386
  2.0 32.9 %fused.1 = f32[2,64,1024]{2,1,0:T(8,128)S(1)} custom-call(bf16[56,64,1024]{2,1,0:T(8,128)(2,1)} %tiles_hbm.1, s32[8,56]{1,0:T(8,128)S(1)} %pad_add_fusion.args_ref, f32[1,56]{1,0:T(1,128)S(1)} %bitcast_convert_fusion.weight_ref), custom_call_target="tpu_custom_call" | custom-call | tf_op jit(solution)/shard_map/fused/pallas_call | solution.py:391
  34.9 0.8 %slice_bitcast_fusion = (f32[64,1024]{1,0:T(8,128)}, f32[64,1024]{1,0:T(8,128)}) fusion(f32[2,64,1024]{2,1,0:T(8,128)S(1)} %fused.1), kind=kLoop, calls=%fused_computation | loop fusion | bytes 1048576 | tf_op jit(solution)/shard_map/squeeze | solution.py:431
